TPU v7x, 32 devices: a whole 2x2x4 slice. The times are simulated.
32 devices in a mesh: groups: 2 (over y), adapter: 4 (over z), tensor: 2 (over x), sub: 2 (over core).
Axes of the slice: x: 2, y: 2, z: 4, core: 2. Of those that a mesh axis runs over, the one named last changes fastest.
Arguments:
- tokens: bfloat16 [8192, 8192], P(('groups', 'adapter'), 'tensor'), parts along dimension 0, may hold values from -6 to 6
- key_value_weight: bfloat16 [8192, 2048], P('tensor', 'sub'), may hold values from -0.0625 to 0.0625
- adapter_down_table: bfloat16 [4, 2, 64, 8192], P('adapter', 'sub', None, 'tensor'), may hold values from -0.0625 to 0.0625
- adapter_up_table: bfloat16 [4, 2, 64, 1024], P('adapter', 'sub'), may hold values from -0.75 to 0.75
- adapter_per_block: int32 [128, 1], P('groups'), parts along dimension 0, may hold values from 0 to 3; in each aligned block of 16 rows (0 to 15, 16 to 31, ...) at most 4 rows name the same one
- adapter_position: int32 [4], replicated, may hold values from 0 to 3, each once
Outputs:
- kv_out: bfloat16 [8192, 2048], P(('groups', 'adapter', 'tensor'), 'sub'), parts along dimension 0
There are 2 independent parts, one for each index of `groups`. A program takes and returns all parts, laid end to end along the dimension named above; an argument that names none is the same for every part. Nothing has to cross between parts.
Inputs may be any that keep to these rules, and one draw needn't show every extreme that they name: `adapter_per_block`: within the 16 blocks of one index of adapter (aligned runs of 16 rows), no adapter is named by more than 4 blocks. A permutation: adapter a is stored at position adapter_position[a] of adapter_down_table and adapter_up_table.
All inputs are finite; a program needn't handle non-finite values.
Results may differ from a plain program's by a relative error of at most 0.0095.
Values may be sent and summed in bfloat16 or wider, within the bound.
A program may use at most 128 MiB of HBM per device.

v0:
```python
import jax
import jax.numpy as jnp
from jax import lax
from jax.sharding import PartitionSpec as P

BLOCK = 64


def shards(
    tokens,
    key_value_weight,
    adapter_down_table,
    adapter_up_table,
    adapter_per_block,
    adapter_position,
):
    tok_rows, feat_cols = tokens.shape
    col_width = key_value_weight.shape[1]
    rank_update = adapter_down_table.shape[2]
    owners = lax.axis_size("adapter")
    tensor_count = lax.axis_size("tensor")
    block_rows = BLOCK
    blocks_dev = tok_rows // block_rows
    out_rows = tok_rows // tensor_count
    out_blocks = out_rows // block_rows
    owner_index = lax.axis_index("adapter")
    tensor_index = lax.axis_index("tensor")
    table_size = adapter_position.shape[0]
    matches = adapter_per_block == jnp.arange(table_size, dtype=jnp.int32)[None, :]
    block_slots = jnp.sum(jnp.where(matches, adapter_position[None, :], 0), axis=1)
    my_slots = lax.dynamic_slice_in_dim(block_slots, owner_index * blocks_dev, blocks_dev)
    onehot = (my_slots[:, None] == jnp.arange(owners, dtype=jnp.int32)[None, :]).astype(jnp.int32)
    blocked = tokens.reshape(blocks_dev, block_rows, feat_cols)
    selector = onehot.astype(jnp.bfloat16)
    columns = selector
    picked = jnp.einsum(
        "bj,jrf->brf",
        columns,
        lax.all_gather(adapter_down_table, "adapter", axis=0, tiled=True)[:, 0],
        preferred_element_type=jnp.float32,
    )
    lowered = jnp.einsum(
        "bxf,brf->bxr", blocked, picked.astype(jnp.bfloat16), preferred_element_type=jnp.float32
    )
    lowered = lowered.reshape(tok_rows, rank_update)
    part = jnp.dot(tokens, key_value_weight, preferred_element_type=jnp.float32).astype(
        jnp.bfloat16
    )
    part = lax.optimization_barrier(part)
    summed_all = lax.psum_scatter(
        part.astype(jnp.float32).astype(jnp.bfloat16), "tensor", scatter_dimension=0, tiled=True
    ).astype(jnp.float32)
    summed = lax.psum(lowered.astype(jnp.bfloat16), "tensor").astype(jnp.float32)
    own_low = lax.dynamic_slice_in_dim(summed, tensor_index * out_rows, out_rows, 0)
    out_slots = lax.dynamic_slice_in_dim(my_slots, tensor_index * out_blocks, out_blocks)
    up_select = (out_slots[:, None] == jnp.arange(owners, dtype=jnp.int32)[None, :]).astype(
        jnp.bfloat16
    )
    columns = up_select
    picked_up = jnp.einsum(
        "bj,jrc->brc",
        columns,
        lax.all_gather(adapter_up_table, "adapter", axis=0, tiled=True)[:, 0],
        preferred_element_type=jnp.float32,
    )
    correction = jnp.einsum(
        "bxr,brc->bxc",
        own_low.reshape(out_blocks, block_rows, rank_update),
        picked_up,
        precision=lax.Precision.HIGHEST,
    )
    return (summed_all + correction.reshape(out_rows, col_width)).astype(jnp.bfloat16)


def solution(mesh):
    placed = (
        P(("groups", "adapter"), "tensor"),
        P("tensor", "sub"),
        P("adapter", "sub", None, "tensor"),
        P("adapter", "sub", None, None),
        P("groups", None),
        P(),
    )
    return jax.shard_map(
        shards,
        mesh=mesh,
        in_specs=placed,
        out_specs=P(("groups", "adapter", "tensor"), "sub"),
        check_vma=False,
    )
```

profile of v0, /device:TPU:0, one launch (start us, length us, event | category | flops | bytes accessed | tf_op | source)
XLA Modules:
  0.0 140.1 jit_solution(7028059838363431938)
XLA Ops:
  6.5 0.0 all-gather.2.cloned.1.call-start
  6.5 0.7 all-gather.2.cloned.1.call-update
  7.3 0.0 all-reduce.2.cloned.1.call-start
  7.3 0.8 select_reduce_fusion
  8.1 0.1 dynamic_slice.11
  8.1 49.5 %all-gather.2.cloned.1.call-done = bf16[4,1,64,4096]{3,2,1,0:T(8,128)(2,1)} async-done(((bf16[1,1,64,4096]{3,2,1,0:T(8,128)(2,1)}), bf16[4,1,64,4096]{3,2,1,0:T(8,128)(2,1)}) %all-gather.2.cloned.1.call-update) | async-done | bytes 2097168 | tf_op jit(solution)/shard_map/all_gather | solution.py:39
  57.6 6.0 %convolution_convert_fusion = bf16[16,64,4096]{2,0,1:T(8,128)(2,1)} fusion(bf16[4,1,64,4096]{3,2,1,0:T(8,128)(2,1)} %all-gather.2.cloned.1.call-done, s32[16]{0:T(128)S(1)} %dynamic_slice.11), kind=kOutput, calls=%fused_computation.2 | convolution fusion | flops 37748928 | bytes 10485824 | tf_op jit(solution)/shard_map/bj,jrf->brf/dot_general | solution.py:36
  63.6 11.3 %fusion.10 = bf16[16,64,64]{1,2,0:T(8,128)(2,1)S(1)} fusion(bf16[16,64,4096]{2,1,0:T(8,128)(2,1)} %bitcast.28, bf16[16,64,4096]{2,0,1:T(8,128)(2,1)} %convolution_convert_fusion), kind=kOutput, calls=%fused_computation.11 | convolution fusion | flops 536936448 | bytes 16908288 | tf_op jit(solution)/shard_map/bxf,brf->bxr/dot_general | solution.py:42
  74.9 0.2 copy.17
  75.1 0.9 convert_element_type.38
  75.9 0.0 all-reduce.2.cloned.1.call-update
  75.9 0.0 copy-start
  76.0 0.0 reduce-scatter.2.cloned.1.call-start
  76.0 14.8 %convolution_convert_fusion.1 = bf16[1024,1024]{1,0:T(8,128)(2,1)} fusion(bf16[1024,4096]{1,0:T(8,128)(2,1)} %param.6, bf16[4096,1024]{1,0:T(8,128)(2,1)} %param.7), kind=kOutput, calls=%fused_computation.9 | convolution fusion | flops 8590983168 | bytes 18874368 | tf_op jit(solution)/shard_map/dot_general | solution.py:46
  90.8 0.0 reduce-scatter.2.cloned.1.call-update
  90.8 0.1 dynamic_slice.14
  90.9 0.0 copy-done
  90.9 15.9 %all_gather.7 = bf16[4,1,64,1024]{3,2,1,0:T(8,128)(2,1)S(1)} all-gather(bf16[1,1,64,1024]{3,2,1,0:T(8,128)(2,1)S(1)} %copy-done), channel_id=1, replica_groups=mesh['groups'=2,'adapter'=4,'tensor'=2,'sub'=2] {'adapter'}, dimensions={0}, use_global_device_ids=true | all-gather | bytes 655360 | tf_op jit(solution)/shard_map/all_gather | solution.py:63
  106.8 0.6 fusion.13
  107.4 0.0 all-reduce.2.cloned.1.call-done
  107.4 0.9 constant_dynamic-slice_fusion
  108.3 0.1 copy.18
  108.4 3.8 %fusion.4 = f32[8,64,1024]{2,1,0:T(8,128)} fusion(bf16[8,64,64]{2,1,0:T(8,128)(2,1)S(1)} %bitcast.27, f32[8,64,1024]{2,0,1:T(8,128)S(1)} %fusion.13), kind=kOutput, calls=%fused_computation.6 | convolution fusion | flops 402653184 | bytes 4259840 | tf_op jit(solution)/shard_map/bxr,brc->bxc/dot_general | solution.py:66
  112.1 18.2 %reduce-scatter.2.cloned.1.call-done = bf16[512,1024]{1,0:T(8,128)(2,1)} async-done(((bf16[1024,1024]{1,0:T(8,128)(2,1)}), bf16[512,1024]{1,0:T(8,128)(2,1)}) %reduce-scatter.2.cloned.1.call-update) | async-done | bytes 1048592 | tf_op jit(solution)/shard_map/reduce_scatter | solution.py:50
  130.4 3.2 %fusion.2 = bf16[512,1024]{1,0:T(8,128)(2,1)} fusion(f32[8,64,1024]{2,1,0:T(8,128)} %fusion.4, bf16[512,1024]{1,0:T(8,128)(2,1)} %reduce-scatter.2.cloned.1.call-done), kind=kLoop, calls=%fused_computation.4 | loop fusion | flops 1572864 | bytes 4194304 | tf_op jit(solution)/shard_map/convert_element_type | solution.py:72
Async XLA Ops:
  6.5 51.1 %all-gather.2.cloned.1.call-start = ((), (), s32[]{:S(2)}) async-start(), calls=%async_computation.2 | async-start | bytes 2621440 | tf_op jit(solution)/shard_map/all_gather | solution.py:39
  7.3 100.1 %all-reduce.2.cloned.1.call-start = ((), (), s32[]{:S(2)}) async-start(), calls=%async_computation.3 | async-start | bytes 262144 | tf_op jit(solution)/shard_map/psum | solution.py:53
  75.9 14.9 %copy-start = (bf16[1,1,64,1024]{3,2,1,0:T(8,128)(2,1)S(1)}, bf16[1,1,64,1024]{3,2,1,0:T(8,128)(2,1)}, u32[]{:S(2)}) copy-start(bf16[1,1,64,1024]{3,2,1,0:T(8,128)(2,1)} %param.9) | copy-start | bytes 393220
  76.0 54.4 %reduce-scatter.2.cloned.1.call-start = ((), (), s32[]{:S(2)}) async-start(), calls=%async_computation.1 | async-start | bytes 3145728 | tf_op jit(solution)/shard_map/reduce_scatter | solution.py:50
Sparse Core Ops, SparseCore 0:
  8.9 48.6 all-gather.1
  76.1 20.1 all-reduce.1
  98.5 31.8 reduce-scatter.1
where the time goes:
time: 140 us
  waiting for transfers between devices  68.4 us (49%)
  matrix products  36.4 us (26%)
  blocking collectives  15.9 us (11%)
  between operations  13.2 us (9%)
  other arithmetic  3.93 us (3%)
  local copies, waits for them, and re-layouts  2.17 us (2%)
    all_gather x1, waiting for transfers between devices, shards(): lax.all_gather(adapter_down_table, 'adapter', axis=0, tiled=True)[:, 0]  49.5 us
    reduce_scatter x1, waiting for transfers between devices, shards(): lax.psum_scatter(part.astype(jnp.float32).astype(jnp.bfloat16), 'tensor',...  18.2 us
    all_gather x1, blocking collectives, shards(): lax.all_gather(adapter_up_table, 'adapter', axis=0, tiled=True)[:, 0]  15.9 us
    dot_general x1, matrix products, shards(): jnp.dot(tokens, key_value_weight, preferred_element_type=jnp.float32)  14.8 us
    dot_general x1, matrix products, shards(): jnp.einsum('bxf,brf->bxr', blocked, picked.astype(jnp.bfloat16), preferre...  11.3 us
    dot_general x1, matrix products, shards(): jnp.einsum('bj,jrf->brf', columns, lax.all_gather(adapter_down_table, 'ad...  6 us
    dot_general x1, matrix products, shards(): jnp.einsum('bxr,brc->bxc', own_low.reshape(out_blocks, block_rows, rank_u...  3.77 us
    convert_element_type x1, other arithmetic, shards(): (summed_all + correction.reshape(out_rows, col_width)).astype(jnp.bfloat16)  3.17 us
  transfers between devices with their start and end apart: 3, of which 2 were waited for; matrix products, arithmetic and copies ran while one was open for 15% of the time, Pallas kernels for 0%

commit v1 on v0

v1 whole, which is shorter than its diff:
```python
import functools

import jax
import jax.numpy as jnp
from jax import lax
from jax.experimental import pallas as pl
from jax.experimental.pallas import tpu as pltpu
from jax.sharding import PartitionSpec as P

BLOCK = 64
LANES = 128
CHUNKS = 4
MESH = pl.DeviceIdType.MESH
F32 = jnp.float32
BF16 = jnp.bfloat16


def kernel(
    sizes,
    tok_hbm, w_hbm, down_hbm, up_hbm, block_adapter, position,
    out_ref,
    tok, wgt, down, up, part, peer_part, own, low, fold, low_send, low_recv, total,
    tok_sem, w_sem, own_sem,
    xs, xr, ls, lr, zs, zr, ys, yr, us, ur, uys, uyr,
):
    owners, groups, tensors, mt, ct = sizes
    rows, feats = tok.shape
    cols = wgt.shape[1]
    rank = down.shape[1]
    wide = owners * rank
    out_rows = rows // tensors
    out_blocks = out_rows // BLOCK
    half_blocks = out_blocks // 2
    half = out_rows // 2
    n_i, n_k = out_rows // mt, cols // ct
    tiles = n_i * n_k
    fq = feats // (groups * CHUNKS)
    cq = cols // groups
    z = lax.axis_index("adapter")
    g = lax.axis_index("groups")
    t = lax.axis_index("tensor")

    def peer(d):
        return lax.rem(t + d, tensors)

    def group(e):
        return lax.rem(g + e, groups)

    order = list(range(1, tensors)) + [0]

    def tok_load(d, i):
        r = pl.ds(pl.multiple_of(peer(d) * out_rows + i * mt, mt), mt)
        return pltpu.make_async_copy(tok_hbm.at[r, :], tok.at[r, :], tok_sem.at[d, i])

    def w_load(k):
        c = pl.ds(pl.multiple_of(k * ct, ct), ct)
        return pltpu.make_async_copy(w_hbm.at[:, c], wgt.at[:, c], w_sem.at[k])

    def own_loads():
        return (
            pltpu.make_async_copy(down_hbm.at[0, 0], down.at[z], own_sem.at[0]),
            pltpu.make_async_copy(up_hbm.at[0, 0], up.at[z], own_sem.at[1]),
        )

    def feat(h, c):
        return pl.ds(pl.multiple_of((h * CHUNKS + c) * fq, fq), fq)

    def ucol(h):
        return pl.ds(pl.multiple_of(h * cq, cq), cq)

    def zcopy(step, j, c, first=False):
        src = down_hbm.at[0, 0, :, feat(g, c)] if first else down.at[j, :, feat(g, c)]
        return pltpu.make_async_remote_copy(
            src_ref=src, dst_ref=down.at[j, :, feat(g, c)],
            send_sem=zs.at[(step + 1) // 2, j, c], recv_sem=zr.at[j, c],
            device_id={"adapter": z + step}, device_id_type=MESH)

    def ycopy(e, j, h, c):
        return pltpu.make_async_remote_copy(
            src_ref=down.at[j, :, feat(h, c)], dst_ref=down.at[j, :, feat(h, c)],
            send_sem=ys.at[e - 1, j, c], recv_sem=yr.at[j, h, c],
            device_id={"groups": group(e)}, device_id_type=MESH)

    def ucopy(step, j, first=False):
        src = up_hbm.at[0, 0, :, ucol(g)] if first else up.at[j, :, ucol(g)]
        return pltpu.make_async_remote_copy(
            src_ref=src, dst_ref=up.at[j, :, ucol(g)],
            send_sem=us.at[(step + 1) // 2, j], recv_sem=ur.at[j],
            device_id={"adapter": z + step}, device_id_type=MESH)

    def uycopy(e, j, h):
        return pltpu.make_async_remote_copy(
            src_ref=up.at[j, :, ucol(h)], dst_ref=up.at[j, :, ucol(h)],
            send_sem=uys.at[e - 1, j], recv_sem=uyr.at[j, h],
            device_id={"groups": group(e)}, device_id_type=MESH)

    def inside(j):
        return (j >= 0) & (j < owners)

    def down_first():
        for c in range(CHUNKS):
            for step in (-1, 1):
                @pl.when(inside(z + step))
                def _():
                    zcopy(step, z, c, True).start()

    def up_first():
        for step in (-1, 1):
            @pl.when(inside(z + step))
            def _():
                ucopy(step, z, True).start()

    def down_on(s, c):
        for side in (-1, 1):
            j = z + side * s

            @pl.when(inside(j))
            def _():
                zcopy(-side, j, c).wait_recv()

                @pl.when(inside(z - side))
                def _():
                    zcopy(-side, j, c).start()
                for e in range(1, groups):
                    ycopy(e, j, g, c).start()

    def up_on(s):
        for side in (-1, 1):
            j = z + side * s

            @pl.when(inside(j))
            def _():
                ucopy(-side, j).wait_recv()

                @pl.when(inside(z - side))
                def _():
                    ucopy(-side, j).start()
                for e in range(1, groups):
                    uycopy(e, j, g).start()

    def tile_at(i, k):
        return (
            pl.ds(pl.multiple_of(i * mt, mt), mt),
            pl.ds(pl.multiple_of(k * ct, ct), ct),
        )

    def xcopy(d, i, k):
        r, c = tile_at(i, k)
        return pltpu.make_async_remote_copy(
            src_ref=part.at[d - 1, r, c], dst_ref=peer_part.at[d - 1, r, c],
            send_sem=xs.at[d - 1, i, k], recv_sem=xr.at[d - 1, i, k],
            device_id={"tensor": peer(d)}, device_id_type=MESH)

    def lcopy(d):
        return pltpu.make_async_remote_copy(
            src_ref=low_send.at[d - 1], dst_ref=low_recv.at[d - 1],
            send_sem=ls.at[d - 1], recv_sem=lr.at[d - 1],
            device_id={"tensor": peer(d)}, device_id_type=MESH)

    tok_load(order[0], 0).start()
    w_load(0).start()
    for k in range(1, n_k):
        w_load(k).start()
    for n, d in enumerate(order):
        for i in range(n_i):
            if n or i:
                tok_load(d, i).start()
    for copy in own_loads():
        copy.start()

    barrier = pltpu.get_barrier_semaphore()
    for step in (-1, 1):
        @pl.when(inside(z + step))
        def _():
            pl.semaphore_signal(barrier, inc=1, device_id={"adapter": z + step}, device_id_type=MESH)
    for e in range(1, groups):
        pl.semaphore_signal(barrier, inc=1, device_id={"groups": group(e)}, device_id_type=MESH)
    for d in range(1, tensors):
        pl.semaphore_signal(barrier, inc=1, device_id={"tensor": peer(d)}, device_id_type=MESH)
    ends = jnp.where(z == 0, 1, 0) + jnp.where(z == owners - 1, 1, 0)
    pl.semaphore_wait(barrier, groups + tensors - ends)
    down_first()

    for n, d in enumerate(order):
        def tile(step, carry, n=n, d=d):
            i, k = step // n_k, step % n_k

            @pl.when(k == 0)
            def _():
                tok_load(d, i).wait()
            if n == 0:
                @pl.when(i == 0)
                def _():
                    w_load(k).wait()
            r, c = tile_at(i, k)
            tr = pl.ds(pl.multiple_of(peer(d) * out_rows + i * mt, mt), mt)
            value = jnp.dot(tok[tr, :], wgt[:, c], preferred_element_type=F32)
            if d:
                part[d - 1, r, c] = value.astype(BF16)
                xcopy(d, i, k).start()
            else:
                own[r, c] = value
            s = 1 if n == tensors - 2 else 2 if n == tensors - 1 else 0
            if 0 < s < owners - 1:
                @pl.when(step >= tiles - CHUNKS)
                def _():
                    down_on(s, step - (tiles - CHUNKS))
            return carry

        lax.fori_loop(0, tiles, tile, 0)
        if n == tensors - 2:
            up_first()
    for copy in own_loads():
        copy.wait()
    if owners > 2:
        up_on(1)
    for s in range(3, owners - 1):
        for c in range(CHUNKS):
            down_on(s, c)
        up_on(s - 1)

    def lower(r, h, c, first=False):
        f = feat(h, c)
        table = down[:, :, f].reshape(wide, fq)
        value = lax.dot_general(
            tok[r, f], table, (((1,), (1,)), ((), ())), preferred_element_type=F32)
        if first:
            low[r, :] = value
        else:
            low[r, :] = low[r, :] + value

    def across(e, c):
        h = group(e)

        def one(j, carry):
            @pl.when(j != z)
            def _():
                ycopy(e, j, h, c).wait_recv()
            return carry

        lax.fori_loop(0, owners, one, 0)

    everything = pl.ds(0, rows)
    jobs = []
    for c in range(CHUNKS):
        jobs.append((0, c))
        if c:
            jobs += [(e, c - 1) for e in range(1, groups)]
    jobs += [(e, CHUNKS - 1) for e in range(1, groups)]
    for n, (e, c) in enumerate(jobs):
        if e == 0:
            if owners > 1:
                down_on(owners - 1, c)
        else:
            across(e, c)
        if n < len(jobs) - 1:
            lower(everything, group(e), c, n == 0)
    if owners > 3:
        up_on(owners - 2)

    lane = lax.broadcasted_iota(jnp.int32, (BLOCK, LANES), 1)
    wide_lane = lax.broadcasted_iota(jnp.int32, (BLOCK, wide), 1) // rank

    def slot(d, b):
        at = z * (rows // BLOCK) + peer(d) * out_blocks + b
        return position[block_adapter[at]]

    def folded(d, b):
        r = pl.ds(pl.multiple_of(peer(d) * out_rows + b * BLOCK, BLOCK), BLOCK)
        kept = jnp.where(wide_lane == slot(d, b), low[r, :], 0.0)
        value = kept[:, :LANES]
        for n in range(1, wide // LANES):
            value = value + kept[:, n * LANES:(n + 1) * LANES]
        return value + pltpu.roll(value, rank, 1)

    e, c = jobs[-1]
    for d in order:
        r = pl.ds(pl.multiple_of(peer(d) * out_rows, out_rows), out_rows)
        lower(r, group(e), c)
        if d:
            for b in range(half_blocks):
                low_send[d - 1, b * BLOCK:(b + 1) * BLOCK, :] = jnp.where(
                    lane < rank, folded(d, b), folded(d, b + half_blocks)).astype(BF16)
            lcopy(d).start()
        else:
            for b in range(out_blocks):
                fold[b * BLOCK:(b + 1) * BLOCK, :] = folded(d, b)

    if owners > 1:
        up_on(owners - 1)
    for e in range(1, groups):
        def one(j, carry, e=e):
            @pl.when(j != z)
            def _():
                uycopy(e, j, group(e)).wait_recv()
            return carry

        lax.fori_loop(0, owners, one, 0)

    for d in range(1, tensors):
        lcopy(d).wait_recv()
    for b in range(half_blocks):
        at = pl.ds(b * BLOCK, BLOCK)
        first, second = fold[at, :], fold[pl.ds((b + half_blocks) * BLOCK, BLOCK), :]
        for d in range(1, tensors):
            got = low_recv[d - 1, at, :].astype(F32)
            other = pltpu.roll(got, rank, 1)
            first = first + jnp.where(lane < rank, got, other)
            second = second + jnp.where(lane < rank, other, got)
        for value, block in ((first, b), (second, b + half_blocks)):
            spread = jnp.concatenate([value] * (wide // LANES), axis=1)
            total[block * BLOCK:(block + 1) * BLOCK, :] = jnp.where(
                wide_lane == slot(0, block), spread, 0.0).astype(BF16)

    def finish(step, carry):
        i, k = step // n_k, step % n_k
        r, c = tile_at(i, k)
        value = own[r, c] + jnp.dot(
            total[r, :], up[:, :, c].reshape(wide, ct), preferred_element_type=F32)
        for d in range(1, tensors):
            xcopy(d, i, k).wait_recv()
            value = value + peer_part[d - 1, r, c].astype(F32)
        out_ref[r, c] = value.astype(BF16)
        return carry

    lax.fori_loop(0, tiles, finish, 0)

    for d in range(1, tensors):
        def left(step, carry, d=d):
            xcopy(d, step // n_k, step % n_k).wait_send()
            return carry

        lax.fori_loop(0, tiles, left, 0)
        lcopy(d).wait_send()

    def sent(j, carry):
        for step in (-1, 1):
            @pl.when(inside(z + step) & (step * (z - j) >= 0))
            def _():
                for c in range(CHUNKS):
                    zcopy(step, j, c).wait_send()
                ucopy(step, j).wait_send()

        @pl.when(j != z)
        def _():
            for e in range(1, groups):
                for c in range(CHUNKS):
                    ycopy(e, j, g, c).wait_send()
                uycopy(e, j, g).wait_send()
        return carry

    lax.fori_loop(0, owners, sent, 0)


def shards(mesh, tokens, weight, down, up, block_adapter, position):
    rows, feats = tokens.shape
    cols = weight.shape[1]
    rank = down.shape[2]
    owners, groups, tensors = (mesh.shape[a] for a in ("adapter", "groups", "tensor"))
    out_rows = rows // tensors
    mt, ct = min(256, out_rows), 256
    n_i, n_k = out_rows // mt, cols // ct
    wide = owners * rank
    peers, others = max(tensors - 1, 1), max(groups - 1, 1)
    dma = pltpu.SemaphoreType.DMA
    hbm = pl.BlockSpec(memory_space=pl.ANY)
    smem = pl.BlockSpec(memory_space=pltpu.SMEM)
    flops = 2 * rows * feats * (cols + wide) + 2 * out_rows * wide * cols
    return pl.pallas_call(
        functools.partial(kernel, (owners, groups, tensors, mt, ct)),
        out_shape=jax.ShapeDtypeStruct((out_rows, cols), BF16),
        in_specs=[hbm, hbm, hbm, hbm, smem, smem],
        out_specs=pl.BlockSpec(memory_space=pltpu.VMEM),
        scratch_shapes=[
            pltpu.VMEM((rows, feats), BF16),
            pltpu.VMEM((feats, cols), BF16),
            pltpu.VMEM((owners, rank, feats), BF16),
            pltpu.VMEM((owners, rank, cols), BF16),
            pltpu.VMEM((peers, out_rows, cols), BF16),
            pltpu.VMEM((peers, out_rows, cols), BF16),
            pltpu.VMEM((out_rows, cols), F32),
            pltpu.VMEM((rows, wide), F32),
            pltpu.VMEM((out_rows, LANES), F32),
            pltpu.VMEM((peers, out_rows // 2, LANES), BF16),
            pltpu.VMEM((peers, out_rows // 2, LANES), BF16),
            pltpu.VMEM((out_rows, wide), BF16),
            dma((tensors, n_i)),
            dma((n_k,)),
            dma((2,)),
            dma((peers, n_i, n_k)),
            dma((peers, n_i, n_k)),
            dma((peers,)),
            dma((peers,)),
            dma((2, owners, CHUNKS)),
            dma((owners, CHUNKS)),
            dma((others, owners, CHUNKS)),
            dma((owners, groups, CHUNKS)),
            dma((2, owners)),
            dma((owners,)),
            dma((others, owners)),
            dma((owners, groups)),
        ],
        compiler_params=pltpu.CompilerParams(
            collective_id=0, has_side_effects=True, vmem_limit_bytes=56 * 2**20),
        cost_estimate=pl.CostEstimate(
            flops=flops, bytes_accessed=2 * (rows * feats + feats * cols), transcendentals=0),
    )(tokens, weight, down, up, block_adapter.reshape(-1), position)


def solution(mesh):
    placed = (
        P(("groups", "adapter"), "tensor"),
        P("tensor", "sub"),
        P("adapter", "sub", None, "tensor"),
        P("adapter", "sub", None, None),
        P("groups", None),
        P(),
    )
    return jax.shard_map(
        functools.partial(shards, mesh),
        mesh=mesh,
        in_specs=placed,
        out_specs=P(("groups", "adapter", "tensor"), "sub"),
        check_vma=False,
    )
```

time: 140 us -> 44.2 us (0.32)
  waiting for transfers between devices: 68.4 us -> 0 us
  Pallas kernels: 0 us -> 41.7 us
  matrix products: 36.4 us -> 0 us
  blocking collectives: 15.9 us -> 0 us
  between operations: 13.2 us -> 0.01 us
  other arithmetic: 3.93 us -> 0 us
    all_gather x1 -> x0, waiting for transfers between devices: 49.5 us -> none  [shards(): lax.all_gather(adapter_down_table, 'adapter', axis=0, tiled=True)[:, 0]]
    pallas_call x0 -> x1, Pallas kernels: none -> 41.7 us  [shards(): pl.pallas_call(functools.partial(kernel, (owners, groups, tensors, mt, ct...]
    dot_general x5 -> x0, matrix products: 36.4 us -> none  [the longest x1 14.8 us: shards(): jnp.dot(tokens, key_value_weight, preferred_element_type=jnp.float32)]
    reduce_scatter x1 -> x0, waiting for transfers between devices: 18.2 us -> none  [shards(): lax.psum_scatter(part.astype(jnp.float32).astype(jnp.bfloat16), 'tensor',...]
    all_gather x1 -> x0, blocking collectives: 15.9 us -> none  [shards(): lax.all_gather(adapter_up_table, 'adapter', axis=0, tiled=True)[:, 0]]
    convert_element_type x1 -> x0, other arithmetic: 3.17 us -> none  [shards(): (summed_all + correction.reshape(out_rows, col_width)).astype(jnp.bfloat16)]
    unnamed x2 -> x1, local copies, waits for them, and re-layouts: 0.01 us -> 2.26 us
  transfers between devices with their start and end apart: 3 -> 0, of which waited for: 2 -> 0; matrix products, arithmetic and copies ran while one was open for 15% -> 0% of each run, Pallas kernels for 0% -> 0%
where the time goes in v1:
time: 44.2 us; the launch traced here: 44 us
  Pallas kernels  41.7 us (94%)
  local copies, waits for them, and re-layouts  2.26 us (5%)
    pallas_call x1, Pallas kernels, shards(): pl.pallas_call(functools.partial(kernel, (owners, groups, tensors, mt, ct...  41.7 us
    unnamed x1, local copies, waits for them, and re-layouts  2.26 us

profile of v1, /device:TPU:0, one launch (start us, length us, event | category | flops | bytes accessed | tf_op | source)
XLA Modules:
  0.0 44.0 jit_solution(12787903794168353559)
XLA Ops:
  0.0 41.7 %shard_map.64 = bf16[512,1024]{1,0:T(8,128)(2,1)} custom-call(bf16[1024,4096]{1,0:T(8,128)(2,1)} %tok_hbm.1, bf16[4096,1024]{1,0:T(8,128)(2,1)} %w_hbm.1, bf16[1,1,64,4096]{3,2,1,0:T(8,128)(2,1)} %down_hbm.1, bf16[1,1,64,1024]{3,2,1,0:T(8,128)(2,1)} %up_hbm.1, s32[64]{0:T(128)} %bitcast.1, s32[4]{0:T(128)} %position.1), custom_call_target="tpu_custom_call" | custom-call | flops 11005853696 | bytes 16777216 | tf_op jit(solution)/shard_map/pallas_call | solution.py:369
  41.7 2.3 %copy.8 = bf16[512,1024]{1,0:T(8,128)(2,1)} copy(bf16[512,1024]{1,0:T(8,128)(2,1)} %shard_map.64) | data formatting | bytes 2097152

commit v2 on v1

--- a/solution.py
+++ b/solution.py
@@ -157,16 +157,17 @@
             send_sem=ls.at[d - 1], recv_sem=lr.at[d - 1],
             device_id={"tensor": peer(d)}, device_id_type=MESH)
 
+    queue = [functools.partial(w_load, k) for k in range(1, n_k)]
+    queue += [
+        functools.partial(tok_load, d, i)
+        for n, d in enumerate(order) for i in range(n_i) if n or i
+    ]
     tok_load(order[0], 0).start()
     w_load(0).start()
-    for k in range(1, n_k):
-        w_load(k).start()
-    for n, d in enumerate(order):
-        for i in range(n_i):
-            if n or i:
-                tok_load(d, i).start()
-    for copy in own_loads():
-        copy.start()
+    queue[0]().start()
+    ahead = n_k - 1
+    groups_of_loads = [queue[1:2]] + [queue[n:n + 1] for n in range(2, ahead + 1)]
+    groups_of_loads.append(queue[ahead + 1:])
 
     barrier = pltpu.get_barrier_semaphore()
     for step in (-1, 1):
@@ -192,6 +193,15 @@
                 @pl.when(i == 0)
                 def _():
                     w_load(k).wait()
+            if n == 0:
+                for at, loads in enumerate(groups_of_loads):
+                    @pl.when(step == at)
+                    def _(loads=loads, at=at):
+                        for load in loads:
+                            load().start()
+                        if at == len(groups_of_loads) - 1:
+                            for copy in own_loads():
+                                copy.start()
             r, c = tile_at(i, k)
             tr = pl.ds(pl.multiple_of(peer(d) * out_rows + i * mt, mt), mt)
             value = jnp.dot(tok[tr, :], wgt[:, c], preferred_element_type=F32)
@@ -200,11 +210,15 @@
                 xcopy(d, i, k).start()
             else:
                 own[r, c] = value
-            s = 1 if n == tensors - 2 else 2 if n == tensors - 1 else 0
-            if 0 < s < owners - 1:
-                @pl.when(step >= tiles - CHUNKS)
-                def _():
-                    down_on(s, step - (tiles - CHUNKS))
+            if owners > 2:
+                if n == tensors - 2:
+                    @pl.when(step >= tiles - CHUNKS)
+                    def _():
+                        down_on(1, step - (tiles - CHUNKS))
+                if n == tensors - 1 and owners > 3:
+                    @pl.when(step >= tiles - CHUNKS)
+                    def _():
+                        down_on(2, step - (tiles - CHUNKS))
             return carry
 
         lax.fori_loop(0, tiles, tile, 0)
@@ -212,7 +226,7 @@
             up_first()
     for copy in own_loads():
         copy.wait()
-    if owners > 2:
+    if owners > 3:
         up_on(1)
     for s in range(3, owners - 1):
         for c in range(CHUNKS):
@@ -241,12 +255,7 @@
         lax.fori_loop(0, owners, one, 0)
 
     everything = pl.ds(0, rows)
-    jobs = []
-    for c in range(CHUNKS):
-        jobs.append((0, c))
-        if c:
-            jobs += [(e, c - 1) for e in range(1, groups)]
-    jobs += [(e, CHUNKS - 1) for e in range(1, groups)]
+    jobs = [(e, c) for e in range(groups) for c in range(CHUNKS)]
     for n, (e, c) in enumerate(jobs):
         if e == 0:
             if owners > 1:
@@ -255,8 +264,8 @@
             across(e, c)
         if n < len(jobs) - 1:
             lower(everything, group(e), c, n == 0)
-    if owners > 3:
-        up_on(owners - 2)
+        if n == CHUNKS - 1 and owners > 2:
+            up_on(owners - 2)
 
     lane = lax.broadcasted_iota(jnp.int32, (BLOCK, LANES), 1)
     wide_lane = lax.broadcasted_iota(jnp.int32, (BLOCK, wide), 1) // rank
@@ -297,6 +306,17 @@
 
         lax.fori_loop(0, owners, one, 0)
 
+    def gather(step, carry):
+        i, k = step // n_k, step % n_k
+        r, c = tile_at(i, k)
+        value = own[r, c]
+        for d in range(1, tensors):
+            xcopy(d, i, k).wait_recv()
+            value = value + peer_part[d - 1, r, c].astype(F32)
+        own[r, c] = value
+        return carry
+
+    lax.fori_loop(0, tiles, gather, 0)
     for d in range(1, tensors):
         lcopy(d).wait_recv()
     for b in range(half_blocks):
@@ -317,9 +337,6 @@
         r, c = tile_at(i, k)
         value = own[r, c] + jnp.dot(
             total[r, :], up[:, :, c].reshape(wide, ct), preferred_element_type=F32)
-        for d in range(1, tensors):
-            xcopy(d, i, k).wait_recv()
-            value = value + peer_part[d - 1, r, c].astype(F32)
         out_ref[r, c] = value.astype(BF16)
         return carry
 
@@ -368,7 +385,7 @@
     flops = 2 * rows * feats * (cols + wide) + 2 * out_rows * wide * cols
     return pl.pallas_call(
         functools.partial(kernel, (owners, groups, tensors, mt, ct)),
-        out_shape=jax.ShapeDtypeStruct((out_rows, cols), BF16),
+        out_shape=pltpu.VMEM((out_rows, cols), BF16),
         in_specs=[hbm, hbm, hbm, hbm, smem, smem],
         out_specs=pl.BlockSpec(memory_space=pltpu.VMEM),
         scratch_shapes=[

time: 44.2 us -> 39.8 us (0.900)
  Pallas kernels: 41.7 us -> 38.7 us
  local copies, waits for them, and re-layouts: 2.26 us -> 0.97 us
    pallas_call x1, Pallas kernels: 41.7 us -> 38.7 us  [shards(): pl.pallas_call(functools.partial(kernel, (owners, groups, tensors, mt, ct...]
    unnamed x1, local copies, waits for them, and re-layouts: 2.26 us -> 0.97 us
where the time goes in v2:
time: 39.8 us; the launch traced here: 39.7 us
  Pallas kernels  38.7 us (97%)
  local copies, waits for them, and re-layouts  0.97 us (2%)
    pallas_call x1, Pallas kernels, shards(): pl.pallas_call(functools.partial(kernel, (owners, groups, tensors, mt, ct...  38.7 us
    unnamed x1, local copies, waits for them, and re-layouts  0.97 us

profile of v2, /device:TPU:0, one launch (start us, length us, event | category | flops | bytes accessed | tf_op | source)
XLA Modules:
  0.0 39.7 jit_solution(11565972100384710343)
XLA Ops:
  0.0 38.7 %shard_map.64 = bf16[512,1024]{1,0:T(8,128)(2,1)S(1)} custom-call(bf16[1024,4096]{1,0:T(8,128)(2,1)} %tok_hbm.1, bf16[4096,1024]{1,0:T(8,128)(2,1)} %w_hbm.1, bf16[1,1,64,4096]{3,2,1,0:T(8,128)(2,1)} %down_hbm.1, bf16[1,1,64,1024]{3,2,1,0:T(8,128)(2,1)} %up_hbm.1, s32[64]{0:T(128)} %bitcast.1, s32[4]{0:T(128)} %position.1), custom_call_target="tpu_custom_call" | custom-call | flops 11005853696 | bytes 16777216 | tf_op jit(solution)/shard_map/pallas_call | solution.py:386
  38.7 1.0 %copy.8 = bf16[512,1024]{1,0:T(8,128)(2,1)} copy(bf16[512,1024]{1,0:T(8,128)(2,1)S(1)} %shard_map.64) | data formatting | bytes 2097152

commit v3 on v2

--- a/solution.py
+++ b/solution.py
@@ -164,9 +164,8 @@
     ]
     tok_load(order[0], 0).start()
     w_load(0).start()
-    queue[0]().start()
     ahead = n_k - 1
-    groups_of_loads = [queue[1:2]] + [queue[n:n + 1] for n in range(2, ahead + 1)]
+    groups_of_loads = [queue[0:2]] + [queue[n:n + 1] for n in range(2, ahead + 1)]
     groups_of_loads.append(queue[ahead + 1:])
 
     barrier = pltpu.get_barrier_semaphore()
@@ -182,6 +181,7 @@
     pl.semaphore_wait(barrier, groups + tensors - ends)
     down_first()
 
+    early = (tiles - CHUNKS) // 2
     for n, d in enumerate(order):
         def tile(step, carry, n=n, d=d):
             i, k = step // n_k, step % n_k
@@ -212,13 +212,13 @@
                 own[r, c] = value
             if owners > 2:
                 if n == tensors - 2:
-                    @pl.when(step >= tiles - CHUNKS)
+                    @pl.when((step >= early) & (step < early + CHUNKS))
                     def _():
-                        down_on(1, step - (tiles - CHUNKS))
+                        down_on(1, step - early)
                 if n == tensors - 1 and owners > 3:
-                    @pl.when(step >= tiles - CHUNKS)
+                    @pl.when((step >= early) & (step < early + CHUNKS))
                     def _():
-                        down_on(2, step - (tiles - CHUNKS))
+                        down_on(2, step - early)
             return carry
 
         lax.fori_loop(0, tiles, tile, 0)
@@ -266,6 +266,8 @@
             lower(everything, group(e), c, n == 0)
         if n == CHUNKS - 1 and owners > 2:
             up_on(owners - 2)
+        if n == len(jobs) - 2 and owners > 1:
+            up_on(owners - 1)
 
     lane = lax.broadcasted_iota(jnp.int32, (BLOCK, LANES), 1)
     wide_lane = lax.broadcasted_iota(jnp.int32, (BLOCK, wide), 1) // rank
@@ -295,8 +297,6 @@
             for b in range(out_blocks):
                 fold[b * BLOCK:(b + 1) * BLOCK, :] = folded(d, b)
 
-    if owners > 1:
-        up_on(owners - 1)
     for e in range(1, groups):
         def one(j, carry, e=e):
             @pl.when(j != z)
@@ -332,15 +332,14 @@
             total[block * BLOCK:(block + 1) * BLOCK, :] = jnp.where(
                 wide_lane == slot(0, block), spread, 0.0).astype(BF16)
 
-    def finish(step, carry):
-        i, k = step // n_k, step % n_k
-        r, c = tile_at(i, k)
-        value = own[r, c] + jnp.dot(
-            total[r, :], up[:, :, c].reshape(wide, ct), preferred_element_type=F32)
-        out_ref[r, c] = value.astype(BF16)
+    def finish(k, carry):
+        c = pl.ds(pl.multiple_of(k * ct, ct), ct)
+        value = own[:, c] + jnp.dot(
+            total[...], up[:, :, c].reshape(wide, ct), preferred_element_type=F32)
+        out_ref[:, c] = value.astype(BF16)
         return carry
 
-    lax.fori_loop(0, tiles, finish, 0)
+    lax.fori_loop(0, n_k, finish, 0)
 
     for d in range(1, tensors):
         def left(step, carry, d=d):

time: 39.8 us -> 39.2 us (0.985)
  Pallas kernels: 38.7 us -> 38 us
    pallas_call x1, Pallas kernels: 38.7 us -> 38 us  [shards(): pl.pallas_call(functools.partial(kernel, (owners, groups, tensors, mt, ct...]
where the time goes in v3:
time: 39.2 us; the launch traced here: 39 us
  Pallas kernels  38 us (97%)
  local copies, waits for them, and re-layouts  0.97 us (2%)
    pallas_call x1, Pallas kernels, shards(): pl.pallas_call(functools.partial(kernel, (owners, groups, tensors, mt, ct...  38 us
    unnamed x1, local copies, waits for them, and re-layouts  0.97 us

profile of v3, /device:TPU:0, one launch (start us, length us, event | category | flops | bytes accessed | tf_op | source)
XLA Modules:
  0.0 39.0 jit_solution(5729735672817902046)
XLA Ops:
  0.0 38.0 %shard_map.64 = bf16[512,1024]{1,0:T(8,128)(2,1)S(1)} custom-call(bf16[1024,4096]{1,0:T(8,128)(2,1)} %tok_hbm.1, bf16[4096,1024]{1,0:T(8,128)(2,1)} %w_hbm.1, bf16[1,1,64,4096]{3,2,1,0:T(8,128)(2,1)} %down_hbm.1, bf16[1,1,64,1024]{3,2,1,0:T(8,128)(2,1)} %up_hbm.1, s32[64]{0:T(128)} %bitcast.1, s32[4]{0:T(128)} %position.1), custom_call_target="tpu_custom_call" | custom-call | flops 11005853696 | bytes 16777216 | tf_op jit(solution)/shard_map/pallas_call | solution.py:385
  38.0 1.0 %copy.8 = bf16[512,1024]{1,0:T(8,128)(2,1)} copy(bf16[512,1024]{1,0:T(8,128)(2,1)S(1)} %shard_map.64) | data formatting | bytes 2097152
